TPU v7x, 256 devices: a whole 4x4x8 slice. The times are simulated.
256 devices in a mesh: seq: 64 (over z, y, core), head: 4 (over x).
Axes of the slice: x: 4, y: 4, z: 8, core: 2. Of those that a mesh axis runs over, the one named last changes fastest.
Arguments:
- hidden_in: bfloat16 [8192, 6144], P('seq', 'head'), may hold values from -60 to 60
- query_rows: bfloat16 [8192, 6144], P('seq', 'head'), may hold values from -6 to 6
- key_rows: bfloat16 [8192, 6144], P('seq', 'head'), may hold values from -6 to 6
- value_rows: bfloat16 [8192, 6144], P('seq', 'head'), may hold values from -6 to 6
- log_decay: float32 [8192, 48], P('seq', 'head'), may hold values from -1 to 0
- expert_ids: int32 [8192, 2], P('seq'), may hold values from 0 to 7, all different within a row; in each aligned block of 128 rows (0 to 127, 128 to 255, ...) at most 40 rows name the same one
- gate_values: float32 [8192, 2], P('seq'), may hold values from 0.2 to 1
- gate_weight: bfloat16 [6144, 36864], P('head', 'seq'), may hold values from -0.078125 to 0.078125
- up_weight: bfloat16 [6144, 36864], P('head', 'seq'), may hold values from -0.078125 to 0.078125
- down_weight: bfloat16 [36864, 6144], P('seq', 'head'), may hold values from -0.09375 to 0.09375
Outputs:
- attended: bfloat16 [8192, 6144], P('seq', 'head')
- mixed: bfloat16 [8192, 6144], P('seq', 'head')
Inputs may be any that keep to these rules, and one draw needn't show every extreme that they name: `expert_ids`: each token names two different experts. The tokens of one index of seq name one expert at most 40 times, and some index of seq names some expert exactly 40 times.
All inputs are finite; a program needn't handle non-finite values.
Results may differ from a plain program's by a relative error of at most 0.0095.
Values may be sent and summed in bfloat16 or wider, within the bound.
A program may use at most 128 MiB of HBM per device.

v0:
```python
import jax
import jax.numpy as jnp
from jax import lax
from jax.sharding import PartitionSpec as P

EXPERTS = 8
CAP = 40


def entering(value, axis, combine, identity):
    peers, position = (lax.axis_size(axis), lax.axis_index(axis))
    everything = jax.tree.map(
        lambda part, kind: lax.all_gather(part.astype(kind), axis),
        value,
        (jnp.bfloat16, jnp.bfloat16),
    )
    start = jax.tree.map(
        lambda part, zero: jnp.broadcast_to(jnp.asarray(zero, part.dtype), part.shape),
        value,
        identity,
    )

    def hop(k, before):
        reached = k < position
        new = combine(
            before, jax.tree.map(lambda part, own: part[k].astype(own.dtype), everything, value)
        )
        return jax.tree.map(lambda a, b: jnp.where(reached, a, b), new, before)

    return lax.fori_loop(0, peers, hop, start)


def combine_states(earlier, later):
    return (earlier[0] + later[0], jnp.exp(later[0])[:, None, None] * earlier[1] + later[1])


def on_device(
    hidden_in,
    query_rows,
    key_rows,
    value_rows,
    log_decay,
    expert_ids,
    gate_values,
    gate_weight,
    up_weight,
    down_weight,
):
    tok_rows, width_part = query_rows.shape
    head_count = log_decay.shape[1]
    head_width = width_part // head_count
    scaling = head_width ** (-0.5)
    query_heads = query_rows.reshape(tok_rows, head_count, head_width)
    key_heads = key_rows.reshape(tok_rows, head_count, head_width)
    value_heads = value_rows.reshape(tok_rows, head_count, head_width)
    cumul = jnp.cumsum(log_decay, axis=0)
    token_offsets = jnp.arange(tok_rows)
    causal = (token_offsets[:, None] >= token_offsets[None, :])[:, :, None]
    spread = jnp.where(causal, cumul[:, None, :] - cumul[None, :, :], 0.0)
    decay_mask = jnp.where(causal, jnp.exp(spread), 0.0)
    scores = jnp.einsum("thd,shd->hts", query_heads, key_heads, preferred_element_type=jnp.float32)
    scores = scores * scaling * jnp.transpose(decay_mask, (2, 0, 1))
    intra = jnp.einsum(
        "hts,shd->thd", scores.astype(jnp.bfloat16), value_heads, preferred_element_type=jnp.float32
    )
    block_total = cumul[-1]
    key_decayed = (
        key_heads.astype(jnp.float32) * jnp.exp(block_total[None, :] - cumul)[:, :, None]
    ).astype(jnp.bfloat16)
    local_state = jnp.einsum(
        "shd,she->hde", key_decayed, value_heads, preferred_element_type=jnp.float32
    )
    identity = (jnp.zeros_like(block_total), jnp.zeros_like(local_state))
    incoming = entering((block_total, local_state), "seq", combine_states, identity)
    state_in = incoming[1].astype(jnp.bfloat16)
    query_decayed = (
        query_heads.astype(jnp.float32) * (scaling * jnp.exp(cumul))[:, :, None]
    ).astype(jnp.bfloat16)
    inter = jnp.einsum("thd,hde->the", query_decayed, state_in, preferred_element_type=jnp.float32)
    mixed_heads = intra + inter
    normed_heads = mixed_heads * lax.rsqrt(
        jnp.mean(mixed_heads * mixed_heads, axis=2, keepdims=True) + 1e-05
    )
    attended = (hidden_in.astype(jnp.float32) + normed_heads.reshape(tok_rows, width_part)).astype(
        jnp.bfloat16
    )
    attended_f = attended.astype(jnp.float32)
    square_sums = lax.psum(jnp.sum(attended_f * attended_f, axis=1), "head")
    full_width = width_part * lax.axis_size("head")
    normed_rows = (attended_f * lax.rsqrt(square_sums / full_width + 1e-06)[:, None]).astype(
        jnp.bfloat16
    )
    seq_count = lax.axis_size("seq")
    group_size = seq_count // EXPERTS
    flat_ids = expert_ids.reshape(-1)
    onehot = (flat_ids[:, None] == jnp.arange(EXPERTS)[None, :]).astype(jnp.int32)
    rank_before = jnp.cumsum(onehot, axis=0) - onehot
    slot_index = jnp.sum(rank_before * onehot, axis=1)
    target = flat_ids * CAP + slot_index
    slot_rows = jnp.arange(EXPERTS * CAP)
    dispatch_table = (slot_rows[:, None] == target[None, :]).reshape(EXPERTS * CAP, tok_rows, 2)
    dispatch_table = jnp.any(dispatch_table, axis=2).astype(jnp.bfloat16)
    packed = jnp.dot(dispatch_table, normed_rows, preferred_element_type=jnp.float32).astype(
        jnp.bfloat16
    )
    outgoing = jnp.broadcast_to(
        packed.reshape(EXPERTS, 1, CAP, width_part), (EXPERTS, group_size, CAP, width_part)
    )
    outgoing = outgoing.reshape(seq_count, CAP, width_part)
    arrived = lax.all_to_all(outgoing, "seq", split_axis=0, concat_axis=0, tiled=True)
    sources, slots_here, features = arrived.shape
    flat_rows = arrived.reshape(sources * slots_here, features)
    pre_gate = jnp.dot(flat_rows, gate_weight, preferred_element_type=jnp.float32)
    pre_up = jnp.dot(flat_rows, up_weight, preferred_element_type=jnp.float32)
    gate_sum = lax.psum_scatter(
        pre_gate.astype(jnp.bfloat16), "head", scatter_dimension=1, tiled=True
    ).astype(jnp.float32)
    up_sum = lax.psum_scatter(
        pre_up.astype(jnp.bfloat16), "head", scatter_dimension=1, tiled=True
    ).astype(jnp.float32)
    activations = (jax.nn.silu(gate_sum) * up_sum).astype(jnp.bfloat16)
    activations = lax.all_gather(activations, "head", axis=1, tiled=True)
    share_out = jnp.dot(activations, down_weight, preferred_element_type=jnp.float32).astype(
        jnp.bfloat16
    )
    share_out = share_out.reshape(sources, slots_here, features)
    returned = lax.all_to_all(share_out, "seq", split_axis=0, concat_axis=0, tiled=True)
    expert_rows = returned.reshape(EXPERTS, group_size, CAP, width_part).astype(jnp.float32)
    expert_rows = jnp.sum(expert_rows, axis=1).reshape(EXPERTS * CAP, width_part)
    picked_rows = jnp.take(expert_rows, target, axis=0).reshape(tok_rows, 2, width_part)
    mixture = jnp.sum(picked_rows * gate_values[:, :, None], axis=1)
    mixed = (attended_f + mixture).astype(jnp.bfloat16)
    return (attended, mixed)


def solution(mesh):
    placed = (
        P("seq", "head"),
        P("seq", "head"),
        P("seq", "head"),
        P("seq", "head"),
        P("seq", "head"),
        P("seq", None),
        P("seq", None),
        P("head", "seq"),
        P("head", "seq"),
        P("seq", "head"),
    )
    return jax.shard_map(
        on_device,
        mesh=mesh,
        in_specs=placed,
        out_specs=(P("seq", "head"), P("seq", "head")),
        check_vma=False,
    )
```

profile of v0, /device:TPU:1, one launch (start us, length us, event | category | flops | bytes accessed | tf_op | source)
XLA Modules:
  0.0 755.8 jit_solution(3395768985060886978)
XLA Ops:
  8.4 1.2 copy.86
  9.7 1.2 copy.92
  12.5 44.3 %all-gather.1 = bf16[64,1,12]{2,1,0:T(2,128)(2,1)S(1)} all-gather(bf16[1,1,12]{2,1,0:T(2,128)(2,1)S(1)} %convert_bitcast_fusion), channel_id=1, replica_groups=mesh['seq'=64,'head'=4] {'seq'}, dimensions={0}, use_global_device_ids=true | all-gather | bytes 1560 | tf_op jit(solution)/shard_map/all_gather | solution.py:13
  56.9 1.9 copy.85
  60.1 2.6 convolution_bitcast_fusion.1
  62.7 75.1 %all-gather.7.cloned.1.call-done = bf16[768,128,128]{2,1,0:T(8,128)(2,1)} async-done(((bf16[12,128,128]{2,1,0:T(8,128)(2,1)}), bf16[768,128,128]{2,1,0:T(8,128)(2,1)}) %all-gather.7.cloned.1.call-update) | async-done | bytes 25165840 | tf_op jit(solution)/shard_map/all_gather | solution.py:13
  137.8 78.1 %while.14 = (s32[]{:T(128)}, f32[12,128,128]{2,1,0:T(8,128)S(1)}, s32[]{:T(128)}, bf16[64,12]{1,0:T(8,128)(2,1)S(1)}, bf16[64,12,128,128]{3,2,1,0:T(8,128)(2,1)}, /*index=5*/s32[]{:T(128)}, s32[]{:T(128)}) while((s32[]{:T(128)}, f32[12,128,128]{2,1,0:T(8,128)S(1)}, s32[]{:T(128)}, bf16[64,12]{1,0:T(8,128)(2,1)S(1)}, ...), condition=%wide.region_2.3_spmd.clone, body=%wide.region_1.2_spmd.clone.sunk | while | flops 983056 | bytes 1966305 | solution.py:30
  137.8 1.2 fusion.46
  139.1 1.2 fusion.46
  140.3 1.2 fusion.46
  141.5 1.2 fusion.46
  142.7 1.2 fusion.46
  143.9 1.2 fusion.46
  145.2 1.2 fusion.46
  215.9 1.5 multiply_reduce_fusion.1
  218.4 1.4 copy.100
  220.0 8.4 %psum.7 = f32[128]{0:T(128)S(1)} all-reduce(f32[128]{0:T(128)S(1)} %get-tuple-element.147), channel_id=1, replica_groups=mesh['seq'=64,'head'=4] {'head'}, use_global_device_ids=true, to_apply=%region_9.10 | all-reduce | flops 128 | bytes 1024 | tf_op jit(solution)/shard_map/psum | solution.py:88
  229.5 181.8 %all_to_all.10 = bf16[64,40,1536]{2,1,0:T(8,128)(2,1)S(1)} all-to-all(bf16[64,40,1536]{2,1,0:T(8,128)(2,1)S(1)} %bitcast.59), channel_id=1, replica_groups=mesh['seq'=64,'head'=4] {'seq'}, dimensions={0} | all-to-all | bytes 15728640 | tf_op jit(solution)/shard_map/all_to_all | solution.py:110
  411.3 3.1 copy-done.1
  414.4 6.2 convolution_convert_fusion.2
  420.6 10.2 %convolution_convert_fusion.1 = bf16[2560,576]{0,1:T(8,128)(2,1)} fusion(bf16[2560,1536]{1,0:T(8,128)(2,1)} %bitcast.62, bf16[1536,576]{0,1:T(8,128)(2,1)} %param.20), kind=kOutput, calls=%fused_computation.6 | convolution fusion | flops 4531322880 | bytes 12582912 | tf_op jit(solution)/shard_map/dot_general | solution.py:114
  431.0 23.7 %reduce-scatter.3.cloned.1.call-done = bf16[2560,144]{0,1:T(8,128)(2,1)} async-done(((bf16[2560,576]{0,1:T(8,128)(2,1)}), bf16[2560,144]{0,1:T(8,128)(2,1)}) %reduce-scatter.3.cloned.1.call-update) | async-done | bytes 737296 | tf_op jit(solution)/shard_map/reduce_scatter | solution.py:115
  454.8 41.7 %reduce-scatter.5.cloned.1.call-done = bf16[2560,144]{0,1:T(8,128)(2,1)} async-done(((bf16[2560,576]{0,1:T(8,128)(2,1)}), bf16[2560,144]{0,1:T(8,128)(2,1)}) %reduce-scatter.5.cloned.1.call-update) | async-done | bytes 737296 | tf_op jit(solution)/shard_map/reduce_scatter | solution.py:118
  496.5 2.7 fusion.5
  499.2 40.3 %all-gather.5.cloned.1.call-done = bf16[2560,576]{0,1:T(8,128)(2,1)} async-done(((bf16[2560,144]{0,1:T(8,128)(2,1)}), bf16[2560,576]{0,1:T(8,128)(2,1)}) %all-gather.5.cloned.1.call-update) | async-done | bytes 2949136 | tf_op jit(solution)/shard_map/all_gather | solution.py:122
  539.5 10.4 %convolution_convert_fusion = bf16[2560,1536]{1,0:T(8,128)(2,1)} fusion(bf16[2560,576]{0,1:T(8,128)(2,1)} %all-gather.5.cloned.1.call-done, bf16[576,1536]{1,0:T(8,128)(2,1)S(1)} %copy-done), kind=kOutput, calls=%fused_computation.5 | convolution fusion | flops 4533780480 | bytes 12582912 | tf_op jit(solution)/shard_map/dot_general | solution.py:123
  549.9 11.0 %all-to-all-start.1 = ((bf16[64,40,1536]{2,1,0:T(8,128)(2,1)}), bf16[64,40,1536]{2,1,0:T(8,128)(2,1)}, u32[]{:S(2)}, u32[]{:S(2)}) async-start(bf16[64,40,1536]{2,1,0:T(8,128)(2,1)} %bitcast.60), calls=%async_computation.3 | async-start | bytes 15728640 | tf_op jit(solution)/shard_map/all_to_all | solution.py:127
  561.5 171.0 %all-to-all-done.1 = bf16[64,40,1536]{2,1,0:T(8,128)(2,1)} async-done(((bf16[64,40,1536]{2,1,0:T(8,128)(2,1)}), bf16[64,40,1536]{2,1,0:T(8,128)(2,1)}, u32[]{:S(2)}, u32[]{:S(2)}) %all-to-all-start.1) | async-done | bytes 7864352 | tf_op jit(solution)/shard_map/all_to_all | solution.py:127
  732.5 5.9 convert_reduce_fusion
  738.4 4.6 gather_fusion
  743.0 2.2 gather.7
  745.3 3.1 multiply_reduce_fusion
  (185 shorter events, 76.0 us)
Async XLA Ops:
  7.2 532.3 %copy-start = (bf16[576,1536]{1,0:T(8,128)(2,1)S(1)}, bf16[576,1536]{1,0:T(8,128)(2,1)}, u32[]{:S(2)}) copy-start(bf16[576,1536]{1,0:T(8,128)(2,1)} %param.21) | copy-start | bytes 5308420
  7.2 130.6 %all-gather.7.cloned.1.call-start = ((), (), s32[]{:S(2)}) async-start(), calls=%async_computation.7 | async-start | bytes 25559040 | tf_op jit(solution)/shard_map/all_gather | solution.py:13
  8.1 4.0 copy-start.6
  12.1 442.7 %reduce-scatter.3.cloned.1.call-start = ((), (), s32[]{:S(2)}) async-start(), calls=%async_computation.4 | async-start | bytes 3686400 | tf_op jit(solution)/shard_map/reduce_scatter | solution.py:115
  137.8 78.1 %copy-start.4 = (bf16[128,1536]{0,1:T(8,128)(2,1)S(1)}, bf16[128,1536]{0,1:T(8,128)(2,1)}, u32[]{:S(2)}) copy-start(bf16[128,1536]{0,1:T(8,128)(2,1)} %copy.85) | copy-start | bytes 1179652
  217.4 2.4 copy-start.5
  220.0 9.5 %copy-start.2 = (bf16[128,1536]{1,0:T(8,128)(2,1)}, bf16[128,1536]{1,0:T(8,128)(2,1)S(1)}, u32[]{:S(2)}) copy-start(bf16[128,1536]{1,0:T(8,128)(2,1)S(1)} %get-tuple-element.148) | copy-start | bytes 1179652
  229.5 184.9 %copy-start.8 = (bf16[1536,576]{0,1:T(8,128)(2,1)S(1)}, bf16[1536,576]{0,1:T(8,128)(2,1)}, u32[]{:S(2)}) copy-start(bf16[1536,576]{0,1:T(8,128)(2,1)} %param.19) | copy-start | bytes 5308420
  411.3 3.1 copy-start.1
  420.6 75.9 %reduce-scatter.5.cloned.1.call-start = ((), (), s32[]{:S(2)}) async-start(), calls=%async_computation.5 | async-start | bytes 3686400 | tf_op jit(solution)/shard_map/reduce_scatter | solution.py:118
  430.8 108.7 %all-gather.5.cloned.1.call-start = ((), (), s32[]{:S(2)}) async-start(), calls=%async_computation.6 | async-start | bytes 3686400 | tf_op jit(solution)/shard_map/all_gather | solution.py:122
  549.9 11.4 %copy-start.7 = (f32[128,2]{0,1:T(2,128)S(1)}, f32[128,2]{0,1:T(2,128)}, u32[]{:S(2)}) copy-start(f32[128,2]{0,1:T(2,128)} %param.18) | copy-start | bytes 3076
  549.9 182.6 %all-to-all-start.1 = ((bf16[64,40,1536]{2,1,0:T(8,128)(2,1)}), bf16[64,40,1536]{2,1,0:T(8,128)(2,1)}, u32[]{:S(2)}, u32[]{:S(2)}) async-start(bf16[64,40,1536]{2,1,0:T(8,128)(2,1)} %bitcast.60), calls=%async_computation.3 | async-start | bytes 15728640 | tf_op jit(solution)/shard_map/all_to_all | solution.py:127
  745.3 3.2 copy-start.3
Sparse Core Ops, SparseCore 0:
  12.2 125.5 all-gather.6
  420.7 34.0 reduce-scatter.2
  457.5 38.9 reduce-scatter.4
  499.3 40.1 all-gather.4
where the time goes:
time: 761 us; the launch traced here: 756 us
  waiting for transfers between devices  352 us (46%)
  blocking collectives  234 us (31%)
  other arithmetic  90.9 us (12%)
  matrix products  32.5 us (4%)
  local copies, waits for them, and re-layouts  18.8 us (2%)
  between operations  14 us (2%)
  starting transfers between devices  11.3 us (1%)
    all_to_all x1, blocking collectives, on_device(): lax.all_to_all(outgoing, 'seq', split_axis=0, concat_axis=0, tiled=True)  182 us
    all_to_all x1, waiting for transfers between devices, on_device(): lax.all_to_all(share_out, 'seq', split_axis=0, concat_axis=0, tiled=True)  171 us
    select_n x64, other arithmetic, hop(): return jax.tree.map(lambda a, b: jnp.where(reached, a, b), new, before)  75.4 us
    all_gather x1, waiting for transfers between devices, entering(): lax.all_gather(part.astype(kind), axis)  75.1 us
    all_gather x1, blocking collectives, entering(): lax.all_gather(part.astype(kind), axis)  44.3 us
    reduce_scatter x1, waiting for transfers between devices, on_device(): lax.psum_scatter(pre_up.astype(jnp.bfloat16), 'head', scatter_dimension=1...  41.7 us
    all_gather x1, waiting for transfers between devices, on_device(): activations = lax.all_gather(activations, 'head', axis=1, tiled=True)  40.3 us
    reduce_scatter x1, waiting for transfers between devices, on_device(): lax.psum_scatter(pre_gate.astype(jnp.bfloat16), 'head', scatter_dimension...  23.7 us
  transfers between devices with their start and end apart: 5, of which 5 were waited for; matrix products, arithmetic and copies ran while one was open for 2% of the time, Pallas kernels for 0%

commit v1 on v0

v1 whole, which is shorter than its diff:
```python
import jax
import jax.numpy as jnp
from jax import lax
from jax.experimental import pallas as pl
from jax.experimental.pallas import tpu as pltpu
from jax.sharding import PartitionSpec as P

MESH = pl.DeviceIdType.MESH
BF = jnp.bfloat16
F32 = jnp.float32

NZ, NY, NX = 8, 4, 4
NP = 8
T = 128
W = 1536
HW = 768
NH = 12
DH = 128
SL = NH * 16
CAP = 40
B = 2 * CAP
CH = 4 * B
NC = 8
FFD = 576
GU = 2 * FFD
AW = 640
SCALE = DH**-0.5
HALVES = ((0, 4, 3, 5), (1, 7, 2, 6))
PLACE = {dz: (h, k) for h, half in enumerate(HALVES) for k, dz in enumerate(half)}


def rcopy(src, dst, ss, rs, dev):
    return pltpu.make_async_remote_copy(
        src_ref=src, dst_ref=dst, send_sem=ss, recv_sem=rs, device_id=dev, device_id_type=MESH
    )


def dot(a, b, dims=((1,), (0,)), precision=None):
    return lax.dot_general(
        a, b, (dims, ((), ())), preferred_element_type=F32, precision=precision
    )


def kernel(
    hid, q, k, v, ld, meta, gw, uw, tw, dw,
    att, mix,
    s_loc, s_in, tot, tot_in, pfx, z_out, z_in, zt_out, zt_in, i_out, i_in,
    intra, qd, sq_out, sq_in, n_half, a_chip, meta_in, code, gate,
    packed, xb, wgu, wdn, acc, part, rs_in, act, d_send, d_keep, d_in, y_in, z_send, z_ret,
    m_out, m_in,
    e1s, e1r, t1s, t1r, e2s, e2r, t2s, t2r, e3s, e3r, sqs, sqr, hs, hr, ms, mr,
    zs, zr, ys, yr, bs, br, rss, rsr, ags, agr, ds, dr, fs, fr, zbs, zbr, os_, or_, wsem,
):
    s = lax.axis_index("seq")
    x = lax.axis_index("head")
    z = s // NP
    p = s % NP
    y = p // 2
    c = p % 2

    def plane(d):
        return (z * NP + (p + d) % NP, x)

    def zpeer(d):
        return (((z + d) % NZ) * NP + p, x)

    def ypeer(d):
        return (z * NP + ((y + d) % NY) * 2 + c, x)

    def xpeer(d):
        return (s, (x + d) % NX)

    sib = (z * NP + y * 2 + (1 - c), x)

    loads = []
    for h in range(2):
        rows = pl.ds(h * HW, HW)
        loads.append((gw.at[rows, pl.ds(0, 512)], wgu.at[h, :, pl.ds(0, 512)]))
        loads.append((uw.at[rows, pl.ds(0, 512)], wgu.at[h, :, pl.ds(512, 512)]))
        loads.append((tw.at[rows, :], wgu.at[h, :, pl.ds(1024, 128)]))
        loads.append((dw.at[:, pl.ds(h * HW, HW)], wdn.at[h, pl.ds(0, FFD), :]))
    loads = [pltpu.make_async_copy(a, b, wsem.at[i]) for i, (a, b) in enumerate(loads)]
    for copy in loads:
        copy.start()

    barrier = pltpu.get_barrier_semaphore()
    for d in range(1, NP):
        pl.semaphore_signal(barrier, inc=1, device_id=plane(d), device_id_type=MESH)
    for d in range(1, NZ):
        pl.semaphore_signal(barrier, inc=1, device_id=zpeer(d), device_id_type=MESH)
    for d in range(1, NX):
        pl.semaphore_signal(barrier, inc=1, device_id=xpeer(d), device_id_type=MESH)

    row = lax.broadcasted_iota(jnp.int32, (T, T), 0)
    col = lax.broadcasted_iota(jnp.int32, (T, T), 1)
    causal = row >= col
    hi = lax.Precision.HIGHEST
    lower = causal.astype(F32)
    upper = (row <= col).astype(F32)
    cumul = dot(lower, ld[...], precision=hi)
    cumul_t = dot(meta[...], upper, precision=hi)
    total = dot(meta[...], jnp.ones((T, T), F32), precision=hi)
    tot[...] = total
    for h in range(NH):
        hd = pl.ds(h * DH, DH)
        keyed = k[:, hd].astype(F32) * jnp.exp(total[h : h + 1, :] - cumul[:, h : h + 1])
        state = dot(keyed.astype(BF), v[:, hd], ((0,), (0,))).astype(BF)
        for j in range(NP):
            s_loc[j, pl.ds(16 * h, 16), :] = state[16 * j : 16 * j + 16, :]

    pl.semaphore_wait(barrier, (NP - 1) + (NZ - 1) + (NX - 1))

    meta_copy = rcopy(meta, meta_in, ms.at[0], mr.at[0], sib)
    meta_copy.start()

    def scan_one(d):
        return rcopy(s_loc.at[(p + d) % NP], s_in.at[p], e1s.at[d - 1], e1r.at[d - 1], plane(d))

    def scan_one_total(d):
        return rcopy(tot, tot_in.at[p], t1s.at[d - 1], t1r.at[d - 1], plane(d))

    for d in range(1, NP):
        scan_one_total(d).start()
        scan_one(d).start()
    s_in[p] = s_loc[p]
    tot_in[p] = tot[...]

    for h in range(NH):
        hd = pl.ds(h * DH, DH)
        own = cumul[:, h : h + 1]
        spread = jnp.where(causal, own - cumul_t[h : h + 1, :], 0.0)
        scores = dot(q[:, hd], k[:, hd], ((1,), (1,))) * SCALE
        weights = jnp.where(causal, scores * jnp.exp(spread), 0.0).astype(BF)
        intra[:, hd] = dot(weights, v[:, hd])
        qd[:, hd] = (q[:, hd].astype(F32) * (SCALE * jnp.exp(own))).astype(BF)

    for d in range(1, NP):
        scan_one_total(d).wait_recv()
        scan_one(d).wait_recv()

    def heads(tile):
        return jnp.concatenate(
            [jnp.broadcast_to(tile[h : h + 1, :], (16, DH)) for h in range(NH)], axis=0
        )

    run = jnp.zeros((SL, DH), F32)
    for j in range(NP):
        pfx[j] = run
        run = heads(jnp.exp(tot_in[j])) * run + s_in[j].astype(F32)
    z_out[...] = run.astype(BF)
    zt_out[...] = sum(tot_in[j] for j in range(NP))

    def scan_two(d):
        return rcopy(z_out, z_in.at[z], e2s.at[d - 1], e2r.at[d - 1], zpeer(d))

    def scan_two_total(d):
        return rcopy(zt_out, zt_in.at[z], t2s.at[d - 1], t2r.at[d - 1], zpeer(d))

    for d in range(1, NZ):
        scan_two_total(d).start()
        scan_two(d).start()
    z_in[z] = z_out[...]
    zt_in[z] = zt_out[...]

    meta_copy.wait_recv()
    expert = lax.broadcasted_iota(jnp.int32, (8, T), 0).astype(F32)
    strict = (row < col).astype(BF)

    def routing(m):
        first, second = expert == m[12:13, :], expert == m[13:14, :]
        chosen = jnp.where(first, 1.0, 0.0) + jnp.where(second, 1.0, 0.0)
        rank = dot(chosen.astype(BF), strict)
        value = jnp.where(first, m[14:15, :], 0.0) + jnp.where(second, m[15:16, :], 0.0)
        return jnp.where(chosen > 0.5, rank, -1000.0), value

    rank, value = routing(meta[...])
    mine = pl.ds(pl.multiple_of(c * T, T), T)
    code[:, mine] = rank + (c * CAP).astype(F32)
    gate[:, mine] = value
    rank, value = routing(meta_in[...])
    other = pl.ds(pl.multiple_of((1 - c) * T, T), T)
    code[:, other] = rank + ((1 - c) * CAP).astype(F32)
    gate[:, other] = value

    for d in range(1, NZ):
        scan_two_total(d).wait_recv()
        scan_two(d).wait_recv()
    run = jnp.zeros((SL, DH), F32)
    for j in range(NZ):
        new = heads(jnp.exp(zt_in[j])) * run + z_in[j].astype(F32)
        run = jnp.where(j < z, new, run)

    def scan_three(d):
        return rcopy(i_out.at[(p + d) % NP], i_in.at[p], e3s.at[d - 1], e3r.at[d - 1], plane(d))

    before = jnp.zeros((16, DH), F32)
    for j in range(NP):
        i_out[j] = (pfx[j] + heads(jnp.exp(before)) * run).astype(BF)
        before = before + tot_in[j]
    for d in range(1, NP):
        scan_three(d).start()
    i_in[p] = i_out[p]
    for d in range(1, NP):
        scan_three(d).wait_recv()

    squares = jnp.zeros((T, DH), F32)
    for h in range(NH):
        hd = pl.ds(h * DH, DH)
        state = jnp.concatenate([i_in[j, pl.ds(16 * h, 16), :] for j in range(NP)], axis=0)
        o = intra[:, hd] + dot(qd[:, hd], state)
        o = o * lax.rsqrt(jnp.mean(o * o, axis=1, keepdims=True) + 1e-05)
        a = (hid[:, hd].astype(F32) + o).astype(BF)
        att[:, hd] = a
        a = a.astype(F32)
        squares = squares + a * a
    sq_out[...] = squares

    def square(d):
        return rcopy(sq_out, sq_in.at[d - 1], sqs.at[d - 1], sqr.at[d - 1], xpeer(d))

    for d in range(1, NX):
        square(d).start()
    for d in range(1, NX):
        square(d).wait_recv()
        squares = squares + sq_in[d - 1]
    scale = lax.rsqrt(jnp.sum(squares, axis=1, keepdims=True) / (W * NX) + 1e-06)
    for h in range(2):
        n_half[h] = (att[:, pl.ds(h * HW, HW)].astype(F32) * scale).astype(BF)

    half_copy = rcopy(n_half.at[1 - c], a_chip.at[c], hs.at[0], hr.at[0], sib)
    half_copy.start()
    a_chip[c] = n_half[c]
    for copy in loads:
        copy.wait()
    for h in range(2):
        wdn[h, pl.ds(FFD, AW - FFD), :] = jnp.zeros((AW - FFD, HW), BF)
    half_copy.wait_recv()

    slot = lax.broadcasted_iota(jnp.int32, (B, 2 * T), 0).astype(F32)

    def dispatch(d):
        half, at = PLACE[(NZ - d) % NZ]
        return rcopy(
            packed.at[d], xb.at[c, 7 * half, pl.ds(B * at, B), :], zs.at[d - 1], zr.at[d - 1], zpeer(d)
        )

    tokens = a_chip[...].reshape(2 * T, HW)
    for d in (4, 5, 3, 7, 1, 6, 2, 0):
        e = (z + d) % NZ
        pick = (slot == code[pl.ds(e, 1), :]).astype(BF)
        rows = dot(pick, tokens).astype(BF)
        if d:
            packed[d] = rows
            dispatch(d).start()
        else:
            xb[c, 0, pl.ds(0, B), :] = rows

    def spread_y(half, d):
        at = NY - d if half == 0 else 4 + (3 - d)
        return rcopy(
            xb.at[c, 7 * half], xb.at[c, at], ys.at[half, d - 1], yr.at[at - 1], ypeer(d)
        )

    def arrive(half):
        for dz in HALVES[half]:
            if dz:
                dispatch(NZ - dz).wait_recv()
        for d in (1, 3, 2):
            spread_y(half, d).start()

    def landed_y(t):
        return rcopy(xb.at[c, t], xb.at[c, t], ys.at[0, 0], yr.at[t - 1], ypeer(1))

    def spread_core(t):
        return rcopy(xb.at[c, t], xb.at[c, t], bs.at[t], br.at[t], sib)

    def landed_core(t):
        return rcopy(xb.at[1 - c, t], xb.at[1 - c, t], bs.at[t], br.at[t], sib)

    def reduce_x(t, d):
        return rcopy(
            part.at[t, (x + d) % NX], rs_in.at[t, d - 1], rss.at[t, d - 1], rsr.at[t, d - 1], xpeer(d)
        )

    def gather_x(t, d):
        mine = act.at[t, x]
        return rcopy(mine, mine, ags.at[t, d - 1], agr.at[t, d - 1], xpeer(d))

    def landed_x(t, d):
        there = act.at[t, (x + NX - d) % NX]
        return rcopy(there, there, ags.at[t, d - 1], agr.at[t, d - 1], xpeer(d))

    def pair_down(t):
        return rcopy(d_send.at[t], d_in.at[t], ds.at[t], dr.at[t], sib)

    def return_y(t):
        dy = (t + t // 4) % NY
        half = t // 4
        return rcopy(
            d_keep.at[t], y_in.at[half, 3 - dy], fs.at[t], fr.at[half, 3 - dy], ypeer(dy)
        )

    def landed_return(half, i):
        return rcopy(y_in.at[half, i], y_in.at[half, i], fs.at[1], fr.at[half, i], ypeer(1))

    def return_z(dz):
        half, at = PLACE[dz]
        return rcopy(
            z_send.at[half, at], z_ret.at[(NZ - dz) % NZ], zbs.at[dz - 1], zbr.at[dz - 1], zpeer(dz)
        )

    def finish(half):
        for i in range(3):
            landed_return(half, i).wait_recv()
        for at, dz in enumerate(HALVES[half]):
            rows = pl.ds(B * at, B)
            whole = d_keep[7 * half, rows, :].astype(F32)
            for i in range(3):
                whole = whole + y_in[half, i, rows, :].astype(F32)
            if dz:
                z_send[half, at] = whole.astype(BF)
                return_z(dz).start()
            else:
                z_ret[0] = whole.astype(BF)

    cuts = [(n, min(256, GU - n)) for n in range(0, GU, 256)]

    def step(t, carry):
        @pl.when(t == 0)
        def _():
            arrive(0)

        @pl.when(t < NC)
        def _():
            @pl.when((t > 0) & (t < NC - 1))
            def _():
                landed_y(t).wait_recv()

            spread_core(t).start()
            for n, w in cuts:
                acc[:, pl.ds(n, w)] = dot(xb[c, t], wgu[c, :, pl.ds(n, w)])
            landed_core(t).wait_recv()
            for n, w in cuts:
                out = acc[:, pl.ds(n, w)] + dot(xb[1 - c, t], wgu[1 - c, :, pl.ds(n, w)])
                out = out.astype(BF)
                for i in range(NX):
                    part[t, i, :, pl.ds(n, w)] = out[B * i : B * i + B, :]
            for d in (2, 1, 3):
                reduce_x(t, d).start()

        @pl.when(t == 0)
        def _():
            arrive(1)

        @pl.when((t >= 1) & (t < NC + 1))
        def _():
            u = t - 1
            for d in range(1, NX):
                reduce_x(u, d).wait_recv()

            def whole(n, w):
                lanes = pl.ds(n, w)
                out = part[u, x, :, lanes].astype(F32)
                for i in range(NX - 1):
                    out = out + rs_in[u, i, :, lanes].astype(F32)
                return out

            g, up = whole(0, 512), whole(512, 512)
            act[u, x, :, pl.ds(0, 512)] = (g / (1.0 + jnp.exp(-g)) * up).astype(BF)
            g = whole(1024, 128)
            up = pltpu.roll(g, 64, 1)
            lane = lax.broadcasted_iota(jnp.int32, (B, 128), 1)
            both = g / (1.0 + jnp.exp(-g)) * up
            act[u, x, :, pl.ds(512, 128)] = jnp.where(lane < 64, both, 0.0).astype(BF)
            for d in (2, 1, 3):
                gather_x(u, d).start()

        @pl.when((t >= 2) & (t < NC + 2))
        def _():
            u = t - 2
            for d in range(1, NX):
                landed_x(u, d).wait_recv()
            a = act[u].reshape(CH, AW)
            for n in range(0, HW, 256):
                d_send[u, :, pl.ds(n, 256)] = dot(a, wdn[1 - c, :, pl.ds(n, 256)]).astype(BF)
            pair_down(u).start()
            for n in range(0, HW, 256):
                d_keep[u, :, pl.ds(n, 256)] = dot(a, wdn[c, :, pl.ds(n, 256)]).astype(BF)
            pair_down(u).wait_recv()
            d_keep[u] = (d_keep[u].astype(F32) + d_in[u].astype(F32)).astype(BF)

            @pl.when((u > 0) & (u < NC - 1))
            def _():
                return_y(u).start()

        @pl.when(t == NC)
        def _():
            finish(0)

        return carry

    lax.fori_loop(0, NC + 2, step, 0)
    finish(1)

    for d in range(1, NZ):
        return_z(d).wait_recv()
    total = jnp.zeros((2 * T, HW), F32)
    for d in range(NZ):
        e = (z + d) % NZ
        pick = jnp.where(slot == code[pl.ds(e, 1), :], gate[pl.ds(e, 1), :], 0.0)
        high = pick.astype(BF)
        low = (pick - high.astype(F32)).astype(BF)
        rows = z_ret[d]
        total = total + dot(high, rows, ((0,), (0,))) + dot(low, rows, ((0,), (0,)))
    m_out[0] = total[:T]
    m_out[1] = total[T:]
    mix_copy = rcopy(m_out.at[1 - c], m_in, os_.at[0], or_.at[0], sib)
    mix_copy.start()
    lanes = pl.ds(pl.multiple_of(c * HW, HW), HW)
    mix[:, lanes] = (att[:, lanes].astype(F32) + m_out[c]).astype(BF)
    mix_copy.wait_recv()
    lanes = pl.ds(pl.multiple_of((1 - c) * HW, HW), HW)
    mix[:, lanes] = (att[:, lanes].astype(F32) + m_in[...]).astype(BF)

    meta_copy.wait_send()
    half_copy.wait_send()
    mix_copy.wait_send()
    for d in range(1, NP):
        scan_one(d).wait_send()
        scan_one_total(d).wait_send()
        scan_three(d).wait_send()
    for d in range(1, NZ):
        scan_two(d).wait_send()
        scan_two_total(d).wait_send()
        dispatch(d).wait_send()
        return_z(d).wait_send()
    for d in range(1, NX):
        square(d).wait_send()
        for half in range(2):
            spread_y(half, d).wait_send()

    def sent(t, carry):
        spread_core(t).wait_send()
        pair_down(t).wait_send()
        for d in range(1, NX):
            reduce_x(t, d).wait_send()
            gather_x(t, d).wait_send()

        @pl.when((t > 0) & (t < NC - 1))
        def _():
            return_y(t).wait_send()

        return carry

    lax.fori_loop(0, NC, sent, 0)


def on_device(hid, q, k, v, ld, ids, gates, gw, uw, dw):
    meta = jnp.concatenate([ld.T, ids.T.astype(F32), gates.T], axis=0)
    tail = jnp.concatenate([gw[:, 512:], uw[:, 512:]], axis=1)
    vmem = pl.BlockSpec(memory_space=pltpu.VMEM)
    anywhere = pl.BlockSpec(memory_space=pl.ANY)
    sem = pltpu.SemaphoreType.DMA
    buffers = [
        ((NP, SL, DH), BF), ((NP, SL, DH), BF), ((16, DH), F32), ((NP, 16, DH), F32),
        ((NP, SL, DH), F32), ((SL, DH), BF), ((NZ, SL, DH), BF), ((16, DH), F32),
        ((NZ, 16, DH), F32), ((NP, SL, DH), BF), ((NP, SL, DH), BF),
        ((T, W), F32), ((T, W), BF), ((T, DH), F32), ((NX - 1, T, DH), F32),
        ((2, T, HW), BF), ((2, T, HW), BF), ((16, T), F32), ((8, 2 * T), F32), ((8, 2 * T), F32),
        ((NZ, B, HW), BF), ((2, NC, CH, HW), BF), ((2, HW, GU), BF), ((2, AW, HW), BF),
        ((CH, GU), F32), ((NC, NX, B, GU), BF), ((NC, NX - 1, B, GU), BF),
        ((NC, NX, B, AW), BF), ((NC, CH, HW), BF), ((NC, CH, HW), BF), ((NC, CH, HW), BF),
        ((2, NY - 1, CH, HW), BF), ((2, 4, B, HW), BF), ((NZ, B, HW), BF),
        ((2, T, HW), F32), ((T, HW), F32),
    ]
    pairs = [
        (7,), (7,), (7,), (7,), (7,), (3,), (1,), (1,),
    ]
    sems = [sem(n) for n in pairs for _ in range(2)]
    sems += [sem((7,)), sem((7,)), sem((2, 3)), sem((6,)), sem((NC,)), sem((NC,))]
    sems += [sem((NC, 3)), sem((NC, 3)), sem((NC, 3)), sem((NC, 3)), sem((NC,)), sem((NC,))]
    sems += [sem((NC,)), sem((2, 3)), sem((7,)), sem((7,)), sem((1,)), sem((1,)), sem((8,))]
    return pl.pallas_call(
        kernel,
        out_shape=(jax.ShapeDtypeStruct((T, W), BF), jax.ShapeDtypeStruct((T, W), BF)),
        in_specs=[vmem] * 6 + [anywhere] * 4,
        out_specs=(vmem, vmem),
        scratch_shapes=[pltpu.VMEM(shape, kind) for shape, kind in buffers] + sems,
        compiler_params=pltpu.CompilerParams(
            collective_id=0, has_side_effects=True, vmem_limit_bytes=60 << 20
        ),
        name="layer",
    )(hid, q, k, v, ld, meta, gw, uw, tail, dw)


def solution(mesh):
    placed = (
        P("seq", "head"),
        P("seq", "head"),
        P("seq", "head"),
        P("seq", "head"),
        P("seq", "head"),
        P("seq", None),
        P("seq", None),
        P("head", "seq"),
        P("head", "seq"),
        P("seq", "head"),
    )
    return jax.shard_map(
        on_device,
        mesh=mesh,
        in_specs=placed,
        out_specs=(P("seq", "head"), P("seq", "head")),
        check_vma=False,
    )
```

time: 761 us -> 225 us (0.30)
  waiting for transfers between devices: 352 us -> 0 us
  blocking collectives: 234 us -> 0 us
  Pallas kernels: 0 us -> 206 us
  other arithmetic: 90.9 us -> 2.96 us
  matrix products: 32.5 us -> 0 us
  between operations: 14 us -> 0.67 us
  starting transfers between devices: 11.3 us -> 0 us
    pallas_call x0 -> x1, Pallas kernels: none -> 206 us  [on_device(): pl.pallas_call(kernel, out_shape=(jax.ShapeDtypeStruct((T, W), BF), jax.S...]
    all_to_all x1 -> x0, blocking collectives: 182 us -> none  [on_device(): lax.all_to_all(outgoing, 'seq', split_axis=0, concat_axis=0, tiled=True)]
    all_to_all x1 -> x0, waiting for transfers between devices: 171 us -> none  [on_device(): lax.all_to_all(share_out, 'seq', split_axis=0, concat_axis=0, tiled=True)]
    all_gather x2 -> x0, waiting for transfers between devices: 115 us -> none  [the longest x1 75.1 us: entering(): lax.all_gather(part.astype(kind), axis)]
    select_n x65 -> x0, other arithmetic: 75.4 us -> none  [the longest x64 75.4 us: hop(): return jax.tree.map(lambda a, b: jnp.where(reached, a, b), new, before)]
    reduce_scatter x2 -> x0, waiting for transfers between devices: 65.4 us -> none  [the longest x1 41.7 us: on_device(): lax.psum_scatter(pre_up.astype(jnp.bfloat16), 'head', scatter_dimension=1...]
    all_gather x1 -> x0, blocking collectives: 44.3 us -> none  [entering(): lax.all_gather(part.astype(kind), axis)]
    dot_general x7 -> x0, matrix products: 32.5 us -> none  [the longest x1 10.4 us: on_device(): jnp.dot(activations, down_weight, preferred_element_type=jnp.float32)]
  transfers between devices with their start and end apart: 5 -> 0, of which waited for: 5 -> 0; matrix products, arithmetic and copies ran while one was open for 2% -> 0% of each run, Pallas kernels for 0% -> 0%
where the time goes in v1:
time: 225 us; the launch traced here: 223 us
  Pallas kernels  206 us (92%)
  local copies, waits for them, and re-layouts  13 us (6%)
  other arithmetic  2.96 us (1%)
    pallas_call x1, Pallas kernels, on_device(): pl.pallas_call(kernel, out_shape=(jax.ShapeDtypeStruct((T, W), BF), jax.S...  206 us
    unnamed x7, local copies, waits for them, and re-layouts  11.9 us

profile of v1, /device:TPU:1, one launch (start us, length us, event | category | flops | bytes accessed | tf_op | source)
XLA Modules:
  0.0 222.8 jit_solution(800509849348709024)
XLA Ops:
  0.6 0.7 convert_bitcast_fusion
  1.3 1.3 pad_maximum_fusion.1.meta
  2.6 1.4 copy.14.ld
  4.1 2.7 %copy.15.gw = bf16[1536,576]{1,0:T(8,128)(2,1)S(1)} copy(bf16[1536,576]{0,1:T(8,128)(2,1)} %param.17) | data formatting | bytes 3538944 | tf_op args[7]
  6.8 0.0 copy-start
  6.8 4.2 %copy.16.uw = bf16[1536,576]{1,0:T(8,128)(2,1)} copy(bf16[1536,576]{0,1:T(8,128)(2,1)} %param.18) | data formatting | bytes 3538944 | tf_op args[8]
  11.1 0.0 copy-done
  11.1 1.0 slice.9
  12.1 1.0 pad_maximum_fusion.tw
  13.0 206.2 %layer.1 = (bf16[128,1536]{1,0:T(8,128)(2,1)}, bf16[128,1536]{1,0:T(8,128)(2,1)}) custom-call(bf16[128,1536]{1,0:T(8,128)(2,1)} %hid.1, bf16[128,1536]{1,0:T(8,128)(2,1)} %q.1, bf16[128,1536]{1,0:T(8,128)(2,1)} %k.1, bf16[128,1536]{1,0:T(8,128)(2,1)} %v.1, f32[128,12]{1,0:T(8,128)} %copy.14.ld, f32[16,128]{1,0:T(8,128)} %pad_maximum_fusion.1.meta, ...), custom_call_target="tpu_custom_call" | custom-call | tf_op jit(solution)/shard_map/layer/pallas_call | solution.py:483
  219.3 1.8 copy.19
  221.1 1.8 copy.20
  (1 shorter events, 0.0 us)
Async XLA Ops:
  6.8 4.3 %copy-start = (bf16[1536,576]{1,0:T(8,128)(2,1)}, bf16[1536,576]{1,0:T(8,128)(2,1)S(1)}, u32[]{:S(2)}) copy-start(bf16[1536,576]{1,0:T(8,128)(2,1)S(1)} %copy.15.gw) | copy-start | bytes 5308420

commit v2 on v1

v2 whole, which is shorter than its diff:
```python
import jax
import jax.numpy as jnp
from jax import lax
from jax.experimental import pallas as pl
from jax.experimental.pallas import tpu as pltpu
from jax.sharding import PartitionSpec as P

MESH = pl.DeviceIdType.MESH
BF = jnp.bfloat16
F32 = jnp.float32

NZ, NY, NX = 8, 4, 4
NP = 8
T = 128
W = 1536
HW = 768
NH = 12
DH = 128
SL = NH * 16
CAP = 40
B = 2 * CAP
CH = NY * B
NC = NZ
FFD = 576
GU = 2 * FFD
AW = 640
SCALE = DH**-0.5
DZ = (0, 1, 6, 2, 5, 3, 4, 7)


def rcopy(src, dst, ss, rs, dev):
    return pltpu.make_async_remote_copy(
        src_ref=src, dst_ref=dst, send_sem=ss, recv_sem=rs, device_id=dev, device_id_type=MESH
    )


def dot(a, b, dims=((1,), (0,)), precision=None):
    return lax.dot_general(
        a, b, (dims, ((), ())), preferred_element_type=F32, precision=precision
    )


def kernel(
    hid, q, k, v, ldt, idt, gt, gw, uw, dw,
    att, mix,
    s_loc, s_in, tot, tot_in, pfx, z_out, z_in, zt_out, zt_in, i_out, i_in,
    intra, qd, sq_out, sq_in, n_half, a_chip, tokens, meta, meta_in, code, gate,
    packed, xb, wgu, wdn, part, rs_in, act, d_send, d_keep, d_in, y_in, z_send, z_ret,
    m_out, m_in,
    e1s, e1r, t1s, t1r, e2s, e2r, t2s, t2r, e3s, e3r, sqs, sqr, hs, hr, ms, mr,
    zs, zr, ys, yr, bs, br, rss, rsr, ags, agr, ds, dr, fs, fr, zbs, zbr, os_, or_, wsem,
):
    s = lax.axis_index("seq")
    x = lax.axis_index("head")
    z = s // NP
    p = s % NP
    y = p // 2
    c = p % 2

    def plane(d):
        return (z * NP + (p + d) % NP, x)

    def zpeer(d):
        return (((z + d) % NZ) * NP + p, x)

    def ypeer(d):
        return (z * NP + ((y + d) % NY) * 2 + c, x)

    def xpeer(d):
        return (s, (x + d) % NX)

    def xcore(dc, dx):
        return (z * NP + y * 2 + (c + dc) % 2, (x + dx) % NX)

    sib = (z * NP + y * 2 + (1 - c), x)

    loads = []
    for h in range(2):
        half = pl.ds(h * HW, HW)
        loads.append((gw.at[pl.ds(0, 512), half], wgu.at[h, pl.ds(0, 512), :]))
        loads.append((uw.at[pl.ds(0, 512), half], wgu.at[h, pl.ds(512, 512), :]))
        loads.append((gw.at[pl.ds(512, 64), half], wgu.at[h, pl.ds(1024, 64), :]))
        loads.append((uw.at[pl.ds(512, 64), half], wgu.at[h, pl.ds(1088, 64), :]))
        loads.append((dw.at[:, half], wdn.at[h, pl.ds(0, FFD), :]))
    loads = [pltpu.make_async_copy(a, b, wsem.at[i]) for i, (a, b) in enumerate(loads)]
    for copy in loads:
        copy.start()

    barrier = pltpu.get_barrier_semaphore()
    for d in range(1, NP):
        pl.semaphore_signal(barrier, inc=1, device_id=plane(d), device_id_type=MESH)
    for d in range(1, NZ):
        pl.semaphore_signal(barrier, inc=1, device_id=zpeer(d), device_id_type=MESH)
    for d in range(1, NX):
        pl.semaphore_signal(barrier, inc=1, device_id=xpeer(d), device_id_type=MESH)
        pl.semaphore_signal(barrier, inc=1, device_id=xcore(1, d), device_id_type=MESH)

    row = lax.broadcasted_iota(jnp.int32, (T, T), 0)
    col = lax.broadcasted_iota(jnp.int32, (T, T), 1)
    causal = row >= col
    hi = lax.Precision.HIGHEST
    lower = causal.astype(F32)
    upper = (row <= col).astype(F32)
    meta[pl.ds(0, NH), :] = ldt[...]
    meta[pl.ds(NH, 2), :] = idt[...].astype(F32)
    meta[pl.ds(NH + 2, 2), :] = gt[...]
    cumul = dot(lower, meta[...], ((1,), (1,)), precision=hi)
    cumul_t = dot(meta[...], upper, precision=hi)
    total = dot(meta[...], jnp.ones((T, T), F32), precision=hi)
    tot[...] = total
    for h in range(NH):
        hd = pl.ds(h * DH, DH)
        keyed = k[:, hd].astype(F32) * jnp.exp(total[h : h + 1, :] - cumul[:, h : h + 1])
        state = dot(keyed.astype(BF), v[:, hd], ((0,), (0,))).astype(BF)
        for j in range(NP):
            s_loc[j, pl.ds(16 * h, 16), :] = state[16 * j : 16 * j + 16, :]

    pl.semaphore_wait(barrier, (NP - 1) + (NZ - 1) + 2 * (NX - 1))

    meta_copy = rcopy(meta, meta_in, ms.at[0], mr.at[0], sib)
    meta_copy.start()

    def scan_one(d):
        return rcopy(s_loc.at[(p + d) % NP], s_in.at[p], e1s.at[d - 1], e1r.at[d - 1], plane(d))

    def scan_one_total(d):
        return rcopy(tot, tot_in.at[p], t1s.at[d - 1], t1r.at[d - 1], plane(d))

    for d in range(1, NP):
        scan_one_total(d).start()
        scan_one(d).start()
    s_in[p] = s_loc[p]
    tot_in[p] = tot[...]

    for h in range(NH):
        hd = pl.ds(h * DH, DH)
        own = cumul[:, h : h + 1]
        spread = jnp.where(causal, own - cumul_t[h : h + 1, :], 0.0)
        scores = dot(q[:, hd], k[:, hd], ((1,), (1,))) * SCALE
        weights = jnp.where(causal, scores * jnp.exp(spread), 0.0).astype(BF)
        intra[:, hd] = dot(weights, v[:, hd])
        qd[:, hd] = (q[:, hd].astype(F32) * (SCALE * jnp.exp(own))).astype(BF)

    for d in range(1, NP):
        scan_one_total(d).wait_recv()
        scan_one(d).wait_recv()

    def heads(tile):
        return jnp.concatenate(
            [jnp.broadcast_to(tile[h : h + 1, :], (16, DH)) for h in range(NH)], axis=0
        )

    run = jnp.zeros((SL, DH), F32)
    for j in range(NP):
        pfx[j] = run
        run = heads(jnp.exp(tot_in[j])) * run + s_in[j].astype(F32)
    z_out[...] = run.astype(BF)
    zt_out[...] = sum(tot_in[j] for j in range(NP))

    def scan_two(d):
        return rcopy(z_out, z_in.at[z], e2s.at[d - 1], e2r.at[d - 1], zpeer(d))

    def scan_two_total(d):
        return rcopy(zt_out, zt_in.at[z], t2s.at[d - 1], t2r.at[d - 1], zpeer(d))

    for d in range(1, NZ):
        scan_two_total(d).start()
        scan_two(d).start()
    z_in[z] = z_out[...]
    zt_in[z] = zt_out[...]

    meta_copy.wait_recv()
    expert = lax.broadcasted_iota(jnp.int32, (8, T), 0).astype(F32)
    strict = (row < col).astype(BF)

    def routing(m):
        first, second = expert == m[12:13, :], expert == m[13:14, :]
        chosen = jnp.where(first, 1.0, 0.0) + jnp.where(second, 1.0, 0.0)
        rank = dot(chosen.astype(BF), strict)
        value = jnp.where(first, m[14:15, :], 0.0) + jnp.where(second, m[15:16, :], 0.0)
        return jnp.where(chosen > 0.5, rank, -1000.0), value

    rank, value = routing(meta[...])
    mine = pl.ds(pl.multiple_of(c * T, T), T)
    code[:, mine] = rank + (c * CAP).astype(F32)
    gate[:, mine] = value
    rank, value = routing(meta_in[...])
    other = pl.ds(pl.multiple_of((1 - c) * T, T), T)
    code[:, other] = rank + ((1 - c) * CAP).astype(F32)
    gate[:, other] = value

    for d in range(1, NZ):
        scan_two_total(d).wait_recv()
        scan_two(d).wait_recv()
    run = jnp.zeros((SL, DH), F32)
    for j in range(NZ):
        new = heads(jnp.exp(zt_in[j])) * run + z_in[j].astype(F32)
        run = jnp.where(j < z, new, run)

    def scan_three(d):
        return rcopy(i_out.at[(p + d) % NP], i_in.at[p], e3s.at[d - 1], e3r.at[d - 1], plane(d))

    before = jnp.zeros((16, DH), F32)
    for j in range(NP):
        i_out[j] = (pfx[j] + heads(jnp.exp(before)) * run).astype(BF)
        before = before + tot_in[j]
    for d in range(1, NP):
        scan_three(d).start()
    i_in[p] = i_out[p]
    for d in range(1, NP):
        scan_three(d).wait_recv()

    squares = jnp.zeros((T, DH), F32)
    for h in range(NH):
        hd = pl.ds(h * DH, DH)
        state = jnp.concatenate([i_in[j, pl.ds(16 * h, 16), :] for j in range(NP)], axis=0)
        o = intra[:, hd] + dot(qd[:, hd], state)
        o = o * lax.rsqrt(jnp.mean(o * o, axis=1, keepdims=True) + 1e-05)
        a = (hid[:, hd].astype(F32) + o).astype(BF)
        att[:, hd] = a
        n_half[h // 6, :, pl.ds(DH * (h % 6), DH)] = a
        a = a.astype(F32)
        squares = squares + a * a
    half_copy = rcopy(n_half.at[1 - c], a_chip, hs.at[0], hr.at[0], sib)
    half_copy.start()

    sq_out[...] = dot(jnp.ones((8, T), F32), squares, ((1,), (1,)), precision=hi)
    others = [(dc, dx) for dc in range(2) for dx in range(NX) if dc or dx]

    def square(dc, dx):
        i = NX * dc + dx - 1
        return rcopy(sq_out, sq_in.at[c, x], sqs.at[i], sqr.at[i], xcore(dc, dx))

    for dc, dx in others:
        square(dc, dx).start()
    sq_in[c, x] = sq_out[...]
    for dc, dx in others:
        square(dc, dx).wait_recv()

    def normed(core, rows):
        whole = sum(sq_in[core, i] for i in range(NX))
        scale = lax.rsqrt(whole / (W * NX) + 1e-06).T[:, 0:1]
        return (rows.astype(F32) * scale).astype(BF)

    tokens[c] = normed(c, n_half[c])
    for h in range(2):
        wdn[h, pl.ds(FFD, AW - FFD), :] = jnp.zeros((AW - FFD, HW), BF)
    half_copy.wait_recv()
    tokens[1 - c] = normed(1 - c, a_chip[...])

    slot = lax.broadcasted_iota(jnp.int32, (B, 2 * T), 0).astype(F32)

    def dispatch(t):
        return rcopy(packed.at[t], xb.at[c, t, 0], zs.at[t], zr.at[t], zpeer(NZ - DZ[t]))

    def distance(t):
        return (1 - t % 2) * ((7 - t // 2) % 7) + (t % 2) * (1 + t // 2 + 3 * (t // 7))

    def landed_z(t):
        return rcopy(xb.at[c, t, 0], xb.at[c, t, 0], zs.at[t], zr.at[t], zpeer(1))

    def along(t):
        return 1 + 2 * (t % 2)

    def spread_y(t, d):
        return rcopy(
            xb.at[c, t, 0], xb.at[c, t, NY - d], ys.at[t, d - 1], yr.at[t, d - 1], ypeer(d)
        )

    def relay_y(t):
        d = along(t)
        return rcopy(xb.at[c, t, NY - d], xb.at[c, t, 2], ys.at[t, 1], yr.at[t, 1], ypeer(d))

    def pass_y(t):
        spread_y(t, along(t)).wait_recv()
        relay_y(t).start()

    def take_z(t):
        landed_z(t).wait_recv()
        spread_y(t, 1).start()
        spread_y(t, 3).start()

    def spread_core(t):
        return rcopy(xb.at[c, t], xb.at[c, t], bs.at[t], br.at[t], sib)

    def landed_core(t):
        return rcopy(xb.at[1 - c, t], xb.at[1 - c, t], bs.at[t], br.at[t], sib)

    def pass_core(t):
        spread_y(t, NY - along(t)).wait_recv()
        relay_y(t).wait_recv()
        spread_core(t).start()

    def reduce_far(t):
        d = along(t)
        return rcopy(part.at[t, (x + 2) % NX], rs_in.at[t, 0], rss.at[t, 0], rsr.at[t, 0], xpeer(d))

    def reduce_near(t):
        d = NX - along(t)
        return rcopy(part.at[t, (x + d) % NX], rs_in.at[t, 1], rss.at[t, 1], rsr.at[t, 1], xpeer(d))

    def reduce_both(t):
        d = along(t)
        return rcopy(part.at[t, (x + d) % NX], rs_in.at[t, 2], rss.at[t, 2], rsr.at[t, 2], xpeer(d))

    def gather_x(t, d):
        mine = act.at[t, x]
        return rcopy(mine, mine, ags.at[t, d - 1], agr.at[t, d - 1], xpeer(d))

    def relay_x(t):
        d = along(t)
        there = act.at[t, (x + NX - d) % NX]
        return rcopy(there, there, ags.at[t, 1], agr.at[t, 1], xpeer(d))

    def pair_down(t):
        return rcopy(d_send.at[t], d_in.at[t], ds.at[t], dr.at[t], sib)

    def return_far(t):
        return rcopy(d_keep.at[t, 2], y_in.at[t, 0], fs.at[t, 0], fr.at[t, 0], ypeer(along(t)))

    def return_near(t):
        d = NY - along(t)
        return rcopy(d_keep.at[t, d], y_in.at[t, 1], fs.at[t, 1], fr.at[t, 1], ypeer(d))

    def return_both(t):
        d = along(t)
        return rcopy(d_keep.at[t, d], y_in.at[t, 2], fs.at[t, 2], fr.at[t, 2], ypeer(d))

    def return_z(t):
        return rcopy(z_send.at[t], z_ret.at[t], zbs.at[t], zbr.at[t], zpeer(distance(t)))

    chip = tokens[...].reshape(2 * T, HW)
    for t in range(NC):
        e = (z + NZ - DZ[t]) % NZ
        pick = (slot == code[pl.ds(e, 1), :]).astype(BF)
        rows = dot(pick, chip).astype(BF)
        if t:
            packed[t] = rows
            dispatch(t).start()
        else:
            xb[c, 0, 0] = rows
            spread_y(0, 1).start()
            spread_y(0, 3).start()
    for copy in loads:
        copy.wait()
    pass_y(0)
    take_z(1)
    pass_core(0)

    cuts = [(n, min(256, GU - n)) for n in range(0, GU, 256)]

    def expand(t):
        landed_core(t).wait_recv()
        own, other = xb[c, t].reshape(CH, HW), xb[1 - c, t].reshape(CH, HW)
        for n, w in cuts:
            out = dot(own, wgu[c, pl.ds(n, w), :], ((1,), (1,)))
            out = out + dot(other, wgu[1 - c, pl.ds(n, w), :], ((1,), (1,)))
            out = out.astype(BF)
            for i in range(NX):
                part[t, i, :, pl.ds(n, w)] = out[B * i : B * i + B, :]
        reduce_far(t).start()
        reduce_near(t).start()

    def reduce(u):
        reduce_far(u).wait_recv()
        there = (x + along(u)) % NX
        both = part[u, there].astype(F32) + rs_in[u, 0].astype(F32)
        part[u, there] = both.astype(BF)
        reduce_both(u).start()

    def activate(u):
        reduce_near(u).wait_recv()
        reduce_both(u).wait_recv()

        def whole(n, w):
            lanes = pl.ds(n, w)
            out = part[u, x, :, lanes].astype(F32)
            for i in (1, 2):
                out = out + rs_in[u, i, :, lanes].astype(F32)
            return out

        g, up = whole(0, 512), whole(512, 512)
        act[u, x, :, pl.ds(0, 512)] = (g / (1.0 + jnp.exp(-g)) * up).astype(BF)
        g = whole(1024, 128)
        up = pltpu.roll(g, 64, 1)
        lane = lax.broadcasted_iota(jnp.int32, (B, 128), 1)
        both = g / (1.0 + jnp.exp(-g)) * up
        act[u, x, :, pl.ds(512, 128)] = jnp.where(lane < 64, both, 0.0).astype(BF)
        gather_x(u, 1).start()
        gather_x(u, 3).start()

    def relay_act(u):
        gather_x(u, along(u)).wait_recv()
        relay_x(u).start()

    def project(u):
        gather_x(u, NX - along(u)).wait_recv()
        relay_x(u).wait_recv()
        a = act[u].reshape(CH, AW)
        for n in range(0, HW, 256):
            out = dot(a, wdn[1 - c, :, pl.ds(n, 256)]).astype(BF)
            d_send[u, :, :, pl.ds(n, 256)] = out.reshape(NY, B, 256)
        pair_down(u).start()
        for n in range(0, HW, 256):
            out = dot(a, wdn[c, :, pl.ds(n, 256)]).astype(BF)
            d_keep[u, :, :, pl.ds(n, 256)] = out.reshape(NY, B, 256)

    def pair(u):
        pair_down(u).wait_recv()
        for i in range(NY):
            both = d_keep[u, i].astype(F32) + d_in[u, i].astype(F32)
            d_keep[u, i] = both.astype(BF)
        return_far(u).start()
        return_near(u).start()

    def fold(u):
        return_far(u).wait_recv()
        d = along(u)
        both = d_keep[u, d].astype(F32) + y_in[u, 0].astype(F32)
        d_keep[u, d] = both.astype(BF)
        return_both(u).start()

    def give(u):
        return_near(u).wait_recv()
        return_both(u).wait_recv()
        whole = d_keep[u, 0].astype(F32)
        for i in (1, 2):
            whole = whole + y_in[u, i].astype(F32)
        whole = whole.astype(BF)

        @pl.when(u == 0)
        def _():
            z_ret[0] = whole

        @pl.when(u > 0)
        def _():
            z_send[u] = whole
            return_z(u).start()

    stages = [
        (give, 7, 0), (fold, 6, 0), (pair, 5, 0), (project, 4, 0), (relay_act, 3, 0), (activate, 2, 0),
        (reduce, 1, 0), (expand, 0, 0), (pass_core, -1, 1), (pass_y, -2, 1), (take_z, -3, 2),
    ]

    def step(t, carry):
        for stage, lag, first in stages:

            @pl.when((t - lag >= first) & (t - lag < NC))
            def _(stage=stage, lag=lag):
                stage(t - lag)

        return carry

    start = min(lag + first for _, lag, first in stages)
    lax.fori_loop(start, NC + max(lag for _, lag, _ in stages), step, 0)

    total = jnp.zeros((2 * T, HW), F32)
    for t in range(NC):
        if t:
            return_z(t).wait_recv()
        e = (z + NZ - DZ[t]) % NZ
        pick = jnp.where(slot == code[pl.ds(e, 1), :], gate[pl.ds(e, 1), :], 0.0)
        high = pick.astype(BF)
        low = (pick - high.astype(F32)).astype(BF)
        rows = z_ret[t]
        total = total + dot(high, rows, ((0,), (0,))) + dot(low, rows, ((0,), (0,)))
    m_out[0] = total[:T]
    m_out[1] = total[T:]
    mix_copy = rcopy(m_out.at[1 - c], m_in, os_.at[0], or_.at[0], sib)
    mix_copy.start()
    lanes = pl.ds(pl.multiple_of(c * HW, HW), HW)
    mix[:, lanes] = (att[:, lanes].astype(F32) + m_out[c]).astype(BF)
    mix_copy.wait_recv()
    lanes = pl.ds(pl.multiple_of((1 - c) * HW, HW), HW)
    mix[:, lanes] = (att[:, lanes].astype(F32) + m_in[...]).astype(BF)

    meta_copy.wait_send()
    half_copy.wait_send()
    mix_copy.wait_send()
    for d in range(1, NP):
        scan_one(d).wait_send()
        scan_one_total(d).wait_send()
        scan_three(d).wait_send()
    for d in range(1, NZ):
        scan_two(d).wait_send()
        scan_two_total(d).wait_send()
    for dc, dx in others:
        square(dc, dx).wait_send()

    def sent(t, carry):
        spread_y(t, 1).wait_send()
        spread_y(t, 3).wait_send()
        relay_y(t).wait_send()
        spread_core(t).wait_send()
        reduce_far(t).wait_send()
        reduce_near(t).wait_send()
        reduce_both(t).wait_send()
        gather_x(t, 1).wait_send()
        gather_x(t, 3).wait_send()
        relay_x(t).wait_send()
        pair_down(t).wait_send()
        return_far(t).wait_send()
        return_near(t).wait_send()
        return_both(t).wait_send()

        @pl.when(t > 0)
        def _():
            landed_z(t).wait_send()
            return_z(t).wait_send()

        return carry

    lax.fori_loop(0, NC, sent, 0)


def hand_over(a, b, a_out, b_out):
    a_out[...] = a[...]
    b_out[...] = b[...]


def on_device(hid, q, k, v, ld, ids, gates, gw, uw, dw):
    vmem = pl.BlockSpec(memory_space=pltpu.VMEM)
    anywhere = pl.BlockSpec(memory_space=pl.ANY)
    sem = pltpu.SemaphoreType.DMA
    buffers = [
        ((NP, SL, DH), BF), ((NP, SL, DH), BF), ((16, DH), F32), ((NP, 16, DH), F32),
        ((NP, SL, DH), F32), ((SL, DH), BF), ((NZ, SL, DH), BF), ((16, DH), F32),
        ((NZ, 16, DH), F32), ((NP, SL, DH), BF), ((NP, SL, DH), BF),
        ((T, W), F32), ((T, W), BF), ((8, T), F32), ((2, NX, 8, T), F32),
        ((2, T, HW), BF), ((T, HW), BF), ((2, T, HW), BF), ((16, T), F32), ((16, T), F32), ((8, 2 * T), F32), ((8, 2 * T), F32),
        ((NZ, B, HW), BF), ((2, NC, NY, B, HW), BF), ((2, GU, HW), BF), ((2, AW, HW), BF),
        ((NC, NX, B, GU), BF), ((NC, NX - 1, B, GU), BF),
        ((NC, NX, B, AW), BF), ((NC, NY, B, HW), BF), ((NC, NY, B, HW), BF), ((NC, NY, B, HW), BF),
        ((NC, 3, B, HW), BF), ((NC, B, HW), BF), ((NC, B, HW), BF),
        ((2, T, HW), F32), ((T, HW), F32),
    ]
    pairs = [
        (7,), (7,), (7,), (7,), (7,), (7,), (1,), (1,),
    ]
    sems = [sem(n) for n in pairs for _ in range(2)]
    three, one = sem((NC, 3)), sem((NC,))
    sems += [one, one, three, three, one, one, three, three, three, three, one, one, three, three]
    sems += [one, one, sem((1,)), sem((1,)), sem((10,))]
    shapes = (jax.ShapeDtypeStruct((T, W), BF), jax.ShapeDtypeStruct((T, W), BF))
    results = pl.pallas_call(
        kernel,
        out_shape=shapes,
        in_specs=[vmem] * 7 + [anywhere] * 3,
        out_specs=(vmem, vmem),
        scratch_shapes=[pltpu.VMEM(shape, kind) for shape, kind in buffers] + sems,
        compiler_params=pltpu.CompilerParams(
            collective_id=0, has_side_effects=True, vmem_limit_bytes=60 << 20
        ),
        name="layer",
    )(hid, q, k, v, ld.T, ids.T, gates.T, gw.T, uw.T, dw)
    return pl.pallas_call(
        hand_over,
        out_shape=shapes,
        in_specs=[vmem] * 2,
        out_specs=(vmem, vmem),
        name="results",
    )(*results)


def solution(mesh):
    placed = (
        P("seq", "head"),
        P("seq", "head"),
        P("seq", "head"),
        P("seq", "head"),
        P("seq", "head"),
        P("seq", None),
        P("seq", None),
        P("head", "seq"),
        P("head", "seq"),
        P("seq", "head"),
    )
    return jax.shard_map(
        on_device,
        mesh=mesh,
        in_specs=placed,
        out_specs=(P("seq", "head"), P("seq", "head")),
        check_vma=False,
    )
```

time: 225 us -> 166 us (0.74); the launches traced: 223 us -> 166 us
  Pallas kernels: 206 us -> 166 us
  local copies, waits for them, and re-layouts: 13 us -> 0 us
  other arithmetic: 2.96 us -> 0 us
    pallas_call x1 -> x2, Pallas kernels: 206 us -> 166 us  [the longest x1 164 us: on_device(): pl.pallas_call(kernel, out_shape=shapes, in_specs=[vmem] * 7 + [anywhere]...]
    unnamed x7 -> x0, local copies, waits for them, and re-layouts: 11.9 us -> none
    concatenate x2 -> x0, other arithmetic: 2.28 us -> none  [the longest x1 1.32 us: on_device(): meta = jnp.concatenate([ld.T, ids.T.astype(F32), gates.T], axis=0)]
where the time goes in v2:
time: 166 us
  Pallas kernels  166 us (100%)
    pallas_call x1, Pallas kernels, on_device(): pl.pallas_call(kernel, out_shape=shapes, in_specs=[vmem] * 7 + [anywhere]...  164 us

profile of v2, /device:TPU:1, one launch (start us, length us, event | category | flops | bytes accessed | tf_op | source)
XLA Modules:
  0.0 166.2 jit_solution(5665551639144776130)
XLA Ops:
  0.6 163.6 %layer.1 = (bf16[128,1536]{1,0:T(8,128)(2,1)}, bf16[128,1536]{1,0:T(8,128)(2,1)}) custom-call(bf16[128,1536]{1,0:T(8,128)(2,1)} %hid.1, bf16[128,1536]{1,0:T(8,128)(2,1)} %q.1, bf16[128,1536]{1,0:T(8,128)(2,1)} %k.1, bf16[128,1536]{1,0:T(8,128)(2,1)} %v.1, f32[12,128]{1,0:T(8,128)} %bitcast.7, s32[2,128]{1,0:T(2,128)} %bitcast.8, f32[2,128]{1,0:T(2,128)} %bitcast.9, ...), custom_call_target="tpu_custom_call" | custom-call | tf_op jit(solution)/shard_map/layer/pallas_call | solution.py:545
  164.2 2.0 %results.1 = (bf16[128,1536]{1,0:T(8,128)(2,1)}, bf16[128,1536]{1,0:T(8,128)(2,1)}) custom-call(bf16[128,1536]{1,0:T(8,128)(2,1)} %get-tuple-element.4.a, bf16[128,1536]{1,0:T(8,128)(2,1)} %get-tuple-element.5.b), custom_call_target="tpu_custom_call" | custom-call | tf_op jit(solution)/shard_map/results/pallas_call | solution.py:556

commit v3 on v2

--- a/solution.py
+++ b/solution.py
@@ -25,6 +25,9 @@
 GU = 2 * FFD
 AW = 640
 SCALE = DH**-0.5
+SUM_WAYS = ((0, 640), (640, 512))
+ACT_WAYS = ((384, 256), (0, 384))
+ROW_WAYS = ((0, 384), (384, 384))
 DZ = (0, 1, 6, 2, 5, 3, 4, 7)
 
 
@@ -44,7 +47,7 @@
     hid, q, k, v, ldt, idt, gt, gw, uw, dw,
     att, mix,
     s_loc, s_in, tot, tot_in, pfx, z_out, z_in, zt_out, zt_in, i_out, i_in,
-    intra, qd, sq_out, sq_in, n_half, a_chip, tokens, meta, meta_in, code, gate,
+    intra, qd, sq_out, sq_in, n_half, a_chip, tokens, picks, meta, meta_in, code, gate,
     packed, xb, wgu, wdn, part, rs_in, act, d_send, d_keep, d_in, y_in, z_send, z_ret,
     m_out, m_in,
     e1s, e1r, t1s, t1r, e2s, e2r, t2s, t2r, e3s, e3r, sqs, sqr, hs, hr, ms, mr,
@@ -189,6 +192,13 @@
     code[:, other] = rank + ((1 - c) * CAP).astype(F32)
     gate[:, other] = value
 
+    slot = lax.broadcasted_iota(jnp.int32, (B, 2 * T), 0).astype(F32)
+    for t in range(NC):
+        e = (z + NZ - DZ[t]) % NZ
+        picks[t] = (slot == code[pl.ds(e, 1), :]).astype(BF)
+    for h in range(2):
+        wdn[h, pl.ds(FFD, AW - FFD), :] = jnp.zeros((AW - FFD, HW), BF)
+
     for d in range(1, NZ):
         scan_two_total(d).wait_recv()
         scan_two(d).wait_recv()
@@ -243,13 +253,9 @@
         return (rows.astype(F32) * scale).astype(BF)
 
     tokens[c] = normed(c, n_half[c])
-    for h in range(2):
-        wdn[h, pl.ds(FFD, AW - FFD), :] = jnp.zeros((AW - FFD, HW), BF)
     half_copy.wait_recv()
     tokens[1 - c] = normed(1 - c, a_chip[...])
 
-    slot = lax.broadcasted_iota(jnp.int32, (B, 2 * T), 0).astype(F32)
-
     def dispatch(t):
         return rcopy(packed.at[t], xb.at[c, t, 0], zs.at[t], zr.at[t], zpeer(NZ - DZ[t]))
 
@@ -259,21 +265,21 @@
     def landed_z(t):
         return rcopy(xb.at[c, t, 0], xb.at[c, t, 0], zs.at[t], zr.at[t], zpeer(1))
 
-    def along(t):
-        return 1 + 2 * (t % 2)
-
     def spread_y(t, d):
+        i = d // 2
+        return rcopy(xb.at[c, t, 0], xb.at[c, t, NY - d], ys.at[t, i], yr.at[t, i], ypeer(d))
+
+    def relay_y(t, way):
+        d, lanes = 1 + 2 * way, pl.ds(*ROW_WAYS[way])
         return rcopy(
-            xb.at[c, t, 0], xb.at[c, t, NY - d], ys.at[t, d - 1], yr.at[t, d - 1], ypeer(d)
+            xb.at[c, t, NY - d, :, lanes], xb.at[c, t, 2, :, lanes],
+            ys.at[t, 2 + way], yr.at[t, 2 + way], ypeer(d),
         )
 
-    def relay_y(t):
-        d = along(t)
-        return rcopy(xb.at[c, t, NY - d], xb.at[c, t, 2], ys.at[t, 1], yr.at[t, 1], ypeer(d))
-
     def pass_y(t):
-        spread_y(t, along(t)).wait_recv()
-        relay_y(t).start()
+        for way in range(2):
+            spread_y(t, 1 + 2 * way).wait_recv()
+            relay_y(t, way).start()
 
     def take_z(t):
         landed_z(t).wait_recv()
@@ -287,53 +293,60 @@
         return rcopy(xb.at[1 - c, t], xb.at[1 - c, t], bs.at[t], br.at[t], sib)
 
     def pass_core(t):
-        spread_y(t, NY - along(t)).wait_recv()
-        relay_y(t).wait_recv()
+        for way in range(2):
+            relay_y(t, way).wait_recv()
         spread_core(t).start()
 
-    def reduce_far(t):
-        d = along(t)
-        return rcopy(part.at[t, (x + 2) % NX], rs_in.at[t, 0], rss.at[t, 0], rsr.at[t, 0], xpeer(d))
-
-    def reduce_near(t):
-        d = NX - along(t)
-        return rcopy(part.at[t, (x + d) % NX], rs_in.at[t, 1], rss.at[t, 1], rsr.at[t, 1], xpeer(d))
-
-    def reduce_both(t):
-        d = along(t)
-        return rcopy(part.at[t, (x + d) % NX], rs_in.at[t, 2], rss.at[t, 2], rsr.at[t, 2], xpeer(d))
+    def sum_x(t, way, d, at, kind):
+        lanes = pl.ds(*SUM_WAYS[way])
+        i = 2 * kind + way
+        return rcopy(
+            part.at[t, at, :, lanes], rs_in.at[t, kind, :, lanes], rss.at[t, i], rsr.at[t, i], xpeer(d)
+        )
+
+    def reduce_far(t, way):
+        return sum_x(t, way, 1 + 2 * way, (x + 2) % NX, 0)
+
+    def reduce_near(t, way):
+        return sum_x(t, way, 3 - 2 * way, (x + 3 - 2 * way) % NX, 1)
+
+    def reduce_both(t, way):
+        return sum_x(t, way, 1 + 2 * way, (x + 1 + 2 * way) % NX, 2)
 
     def gather_x(t, d):
         mine = act.at[t, x]
-        return rcopy(mine, mine, ags.at[t, d - 1], agr.at[t, d - 1], xpeer(d))
-
-    def relay_x(t):
-        d = along(t)
-        there = act.at[t, (x + NX - d) % NX]
-        return rcopy(there, there, ags.at[t, 1], agr.at[t, 1], xpeer(d))
+        return rcopy(mine, mine, ags.at[t, d // 2], agr.at[t, d // 2], xpeer(d))
+
+    def relay_x(t, way):
+        d = 1 + 2 * way
+        there = act.at[t, (x + NX - d) % NX, :, pl.ds(*ACT_WAYS[way])]
+        return rcopy(there, there, ags.at[t, 2 + way], agr.at[t, 2 + way], xpeer(d))
 
     def pair_down(t):
         return rcopy(d_send.at[t], d_in.at[t], ds.at[t], dr.at[t], sib)
 
-    def return_far(t):
-        return rcopy(d_keep.at[t, 2], y_in.at[t, 0], fs.at[t, 0], fr.at[t, 0], ypeer(along(t)))
-
-    def return_near(t):
-        d = NY - along(t)
-        return rcopy(d_keep.at[t, d], y_in.at[t, 1], fs.at[t, 1], fr.at[t, 1], ypeer(d))
-
-    def return_both(t):
-        d = along(t)
-        return rcopy(d_keep.at[t, d], y_in.at[t, 2], fs.at[t, 2], fr.at[t, 2], ypeer(d))
+    def sum_y(t, way, d, at, kind):
+        lanes = pl.ds(*ROW_WAYS[way])
+        i = 2 * kind + way
+        return rcopy(
+            d_keep.at[t, at, :, lanes], y_in.at[t, kind, :, lanes], fs.at[t, i], fr.at[t, i], ypeer(d)
+        )
+
+    def return_far(t, way):
+        return sum_y(t, way, 1 + 2 * way, 2, 0)
+
+    def return_near(t, way):
+        return sum_y(t, way, 3 - 2 * way, 3 - 2 * way, 1)
+
+    def return_both(t, way):
+        return sum_y(t, way, 1 + 2 * way, 1 + 2 * way, 2)
 
     def return_z(t):
         return rcopy(z_send.at[t], z_ret.at[t], zbs.at[t], zbr.at[t], zpeer(distance(t)))
 
     chip = tokens[...].reshape(2 * T, HW)
     for t in range(NC):
-        e = (z + NZ - DZ[t]) % NZ
-        pick = (slot == code[pl.ds(e, 1), :]).astype(BF)
-        rows = dot(pick, chip).astype(BF)
+        rows = dot(picks[t], chip).astype(BF)
         if t:
             packed[t] = rows
             dispatch(t).start()
@@ -358,19 +371,23 @@
             out = out.astype(BF)
             for i in range(NX):
                 part[t, i, :, pl.ds(n, w)] = out[B * i : B * i + B, :]
-        reduce_far(t).start()
-        reduce_near(t).start()
+        for way in range(2):
+            reduce_far(t, way).start()
+        for way in range(2):
+            reduce_near(t, way).start()
 
     def reduce(u):
-        reduce_far(u).wait_recv()
-        there = (x + along(u)) % NX
-        both = part[u, there].astype(F32) + rs_in[u, 0].astype(F32)
-        part[u, there] = both.astype(BF)
-        reduce_both(u).start()
+        for way in range(2):
+            there, lanes = (x + 1 + 2 * way) % NX, pl.ds(*SUM_WAYS[way])
+            reduce_far(u, way).wait_recv()
+            both = part[u, there, :, lanes].astype(F32) + rs_in[u, 0, :, lanes].astype(F32)
+            part[u, there, :, lanes] = both.astype(BF)
+            reduce_both(u, way).start()
 
     def activate(u):
-        reduce_near(u).wait_recv()
-        reduce_both(u).wait_recv()
+        for way in range(2):
+            reduce_near(u, way).wait_recv()
+            reduce_both(u, way).wait_recv()
 
         def whole(n, w):
             lanes = pl.ds(n, w)
@@ -390,12 +407,13 @@
         gather_x(u, 3).start()
 
     def relay_act(u):
-        gather_x(u, along(u)).wait_recv()
-        relay_x(u).start()
+        for way in range(2):
+            gather_x(u, 1 + 2 * way).wait_recv()
+            relay_x(u, way).start()
 
     def project(u):
-        gather_x(u, NX - along(u)).wait_recv()
-        relay_x(u).wait_recv()
+        for way in range(2):
+            relay_x(u, way).wait_recv()
         a = act[u].reshape(CH, AW)
         for n in range(0, HW, 256):
             out = dot(a, wdn[1 - c, :, pl.ds(n, 256)]).astype(BF)
@@ -410,19 +428,23 @@
         for i in range(NY):
             both = d_keep[u, i].astype(F32) + d_in[u, i].astype(F32)
             d_keep[u, i] = both.astype(BF)
-        return_far(u).start()
-        return_near(u).start()
+        for way in range(2):
+            return_far(u, way).start()
+        for way in range(2):
+            return_near(u, way).start()
 
     def fold(u):
-        return_far(u).wait_recv()
-        d = along(u)
-        both = d_keep[u, d].astype(F32) + y_in[u, 0].astype(F32)
-        d_keep[u, d] = both.astype(BF)
-        return_both(u).start()
+        for way in range(2):
+            d, lanes = 1 + 2 * way, pl.ds(*ROW_WAYS[way])
+            return_far(u, way).wait_recv()
+            both = d_keep[u, d, :, lanes].astype(F32) + y_in[u, 0, :, lanes].astype(F32)
+            d_keep[u, d, :, lanes] = both.astype(BF)
+            return_both(u, way).start()
 
     def give(u):
-        return_near(u).wait_recv()
-        return_both(u).wait_recv()
+        for way in range(2):
+            return_near(u, way).wait_recv()
+            return_both(u, way).wait_recv()
         whole = d_keep[u, 0].astype(F32)
         for i in (1, 2):
             whole = whole + y_in[u, i].astype(F32)
@@ -437,31 +459,36 @@
             z_send[u] = whole
             return_z(u).start()
 
+    def lead(t):
+        pass_y(t + 1)
+        take_z(t + 2)
+
+    end = NC - 1
     stages = [
-        (give, 7, 0), (fold, 6, 0), (pair, 5, 0), (project, 4, 0), (relay_act, 3, 0), (activate, 2, 0),
-        (reduce, 1, 0), (expand, 0, 0), (pass_core, -1, 1), (pass_y, -2, 1), (take_z, -3, 2),
+        (give, 7, 0, end), (fold, 6, 0, end), (pair, 5, 0, end), (project, 4, 0, end),
+        (relay_act, 3, 0, end), (activate, 2, 0, end), (reduce, 1, 0, end), (expand, 0, 0, end),
+        (lead, 0, 0, 0), (pass_core, -1, 1, end), (pass_y, -2, 2, end), (take_z, -3, 3, end),
     ]
 
     def step(t, carry):
-        for stage, lag, first in stages:
-
-            @pl.when((t - lag >= first) & (t - lag < NC))
+        for stage, lag, first, last in stages:
+
+            @pl.when((t - lag >= first) & (t - lag <= last))
             def _(stage=stage, lag=lag):
                 stage(t - lag)
 
         return carry
 
-    start = min(lag + first for _, lag, first in stages)
-    lax.fori_loop(start, NC + max(lag for _, lag, _ in stages), step, 0)
+    lax.fori_loop(0, NC + 7, step, 0)
 
     total = jnp.zeros((2 * T, HW), F32)
     for t in range(NC):
-        if t:
-            return_z(t).wait_recv()
         e = (z + NZ - DZ[t]) % NZ
         pick = jnp.where(slot == code[pl.ds(e, 1), :], gate[pl.ds(e, 1), :], 0.0)
         high = pick.astype(BF)
         low = (pick - high.astype(F32)).astype(BF)
+        if t:
+            return_z(t).wait_recv()
         rows = z_ret[t]
         total = total + dot(high, rows, ((0,), (0,))) + dot(low, rows, ((0,), (0,)))
     m_out[0] = total[:T]
@@ -490,18 +517,19 @@
     def sent(t, carry):
         spread_y(t, 1).wait_send()
         spread_y(t, 3).wait_send()
-        relay_y(t).wait_send()
         spread_core(t).wait_send()
-        reduce_far(t).wait_send()
-        reduce_near(t).wait_send()
-        reduce_both(t).wait_send()
         gather_x(t, 1).wait_send()
         gather_x(t, 3).wait_send()
-        relay_x(t).wait_send()
         pair_down(t).wait_send()
-        return_far(t).wait_send()
-        return_near(t).wait_send()
-        return_both(t).wait_send()
+        for way in range(2):
+            relay_y(t, way).wait_send()
+            reduce_far(t, way).wait_send()
+            reduce_near(t, way).wait_send()
+            reduce_both(t, way).wait_send()
+            relay_x(t, way).wait_send()
+            return_far(t, way).wait_send()
+            return_near(t, way).wait_send()
+            return_both(t, way).wait_send()
 
         @pl.when(t > 0)
         def _():
@@ -527,7 +555,7 @@
         ((NP, SL, DH), F32), ((SL, DH), BF), ((NZ, SL, DH), BF), ((16, DH), F32),
         ((NZ, 16, DH), F32), ((NP, SL, DH), BF), ((NP, SL, DH), BF),
         ((T, W), F32), ((T, W), BF), ((8, T), F32), ((2, NX, 8, T), F32),
-        ((2, T, HW), BF), ((T, HW), BF), ((2, T, HW), BF), ((16, T), F32), ((16, T), F32), ((8, 2 * T), F32), ((8, 2 * T), F32),
+        ((2, T, HW), BF), ((T, HW), BF), ((2, T, HW), BF), ((NZ, B, 2 * T), BF), ((16, T), F32), ((16, T), F32), ((8, 2 * T), F32), ((8, 2 * T), F32),
         ((NZ, B, HW), BF), ((2, NC, NY, B, HW), BF), ((2, GU, HW), BF), ((2, AW, HW), BF),
         ((NC, NX, B, GU), BF), ((NC, NX - 1, B, GU), BF),
         ((NC, NX, B, AW), BF), ((NC, NY, B, HW), BF), ((NC, NY, B, HW), BF), ((NC, NY, B, HW), BF),
@@ -538,8 +566,8 @@
         (7,), (7,), (7,), (7,), (7,), (7,), (1,), (1,),
     ]
     sems = [sem(n) for n in pairs for _ in range(2)]
-    three, one = sem((NC, 3)), sem((NC,))
-    sems += [one, one, three, three, one, one, three, three, three, three, one, one, three, three]
+    one, four, six = sem((NC,)), sem((NC, 4)), sem((NC, 6))
+    sems += [one, one, four, four, one, one, six, six, four, four, one, one, six, six]
     sems += [one, one, sem((1,)), sem((1,)), sem((10,))]
     shapes = (jax.ShapeDtypeStruct((T, W), BF), jax.ShapeDtypeStruct((T, W), BF))
     results = pl.pallas_call(

time: 166 us -> 163 us (0.982)
  Pallas kernels: 166 us -> 162 us
    pallas_call x1, Pallas kernels: 164 us -> 160 us  [on_device(): pl.pallas_call(kernel, out_shape=shapes, in_specs=[vmem] * 7 + [anywhere]...]
where the time goes in v3:
time: 163 us
  Pallas kernels  162 us (99%)
    pallas_call x1, Pallas kernels, on_device(): pl.pallas_call(kernel, out_shape=shapes, in_specs=[vmem] * 7 + [anywhere]...  160 us

profile of v3, /device:TPU:1, one launch (start us, length us, event | category | flops | bytes accessed | tf_op | source)
XLA Modules:
  0.0 162.9 jit_solution(11892773666285617164)
XLA Ops:
  0.6 160.2 %layer.1 = (bf16[128,1536]{1,0:T(8,128)(2,1)}, bf16[128,1536]{1,0:T(8,128)(2,1)}) custom-call(bf16[128,1536]{1,0:T(8,128)(2,1)} %hid.1, bf16[128,1536]{1,0:T(8,128)(2,1)} %q.1, bf16[128,1536]{1,0:T(8,128)(2,1)} %k.1, bf16[128,1536]{1,0:T(8,128)(2,1)} %v.1, f32[12,128]{1,0:T(8,128)} %bitcast.7, s32[2,128]{1,0:T(2,128)} %bitcast.8, f32[2,128]{1,0:T(2,128)} %bitcast.9, ...), custom_call_target="tpu_custom_call" | custom-call | tf_op jit(solution)/shard_map/layer/pallas_call | solution.py:573
  160.9 2.0 %results.1 = (bf16[128,1536]{1,0:T(8,128)(2,1)}, bf16[128,1536]{1,0:T(8,128)(2,1)}) custom-call(bf16[128,1536]{1,0:T(8,128)(2,1)} %get-tuple-element.4.a, bf16[128,1536]{1,0:T(8,128)(2,1)} %get-tuple-element.5.b), custom_call_target="tpu_custom_call" | custom-call | tf_op jit(solution)/shard_map/results/pallas_call | solution.py:584

commit v4 on v3

--- a/solution.py
+++ b/solution.py
@@ -166,9 +166,11 @@
     def scan_two_total(d):
         return rcopy(zt_out, zt_in.at[z], t2s.at[d - 1], t2r.at[d - 1], zpeer(d))
 
-    for d in range(1, NZ):
+    farthest = (4, 3, 5, 2, 6, 1, 7)
+    for d in farthest:
+        scan_two(d).start()
+    for d in farthest:
         scan_two_total(d).start()
-        scan_two(d).start()
     z_in[z] = z_out[...]
     zt_in[z] = zt_out[...]
 

time: 163 us -> 164 us (level)
  Pallas kernels: 162 us -> 164 us
where the time goes in v4:
time: 164 us
  Pallas kernels  164 us (100%)
    pallas_call x1, Pallas kernels, on_device(): pl.pallas_call(kernel, out_shape=shapes, in_specs=[vmem] * 7 + [anywhere]...  162 us

profile of v4, /device:TPU:1, one launch (start us, length us, event | category | flops | bytes accessed | tf_op | source)
XLA Modules:
  0.0 164.3 jit_solution(2147359200541462101)
XLA Ops:
  0.6 161.7 %layer.1 = (bf16[128,1536]{1,0:T(8,128)(2,1)}, bf16[128,1536]{1,0:T(8,128)(2,1)}) custom-call(bf16[128,1536]{1,0:T(8,128)(2,1)} %hid.1, bf16[128,1536]{1,0:T(8,128)(2,1)} %q.1, bf16[128,1536]{1,0:T(8,128)(2,1)} %k.1, bf16[128,1536]{1,0:T(8,128)(2,1)} %v.1, f32[12,128]{1,0:T(8,128)} %bitcast.7, s32[2,128]{1,0:T(2,128)} %bitcast.8, f32[2,128]{1,0:T(2,128)} %bitcast.9, ...), custom_call_target="tpu_custom_call" | custom-call | tf_op jit(solution)/shard_map/layer/pallas_call | solution.py:575
  162.3 2.0 %results.1 = (bf16[128,1536]{1,0:T(8,128)(2,1)}, bf16[128,1536]{1,0:T(8,128)(2,1)}) custom-call(bf16[128,1536]{1,0:T(8,128)(2,1)} %get-tuple-element.4.a, bf16[128,1536]{1,0:T(8,128)(2,1)} %get-tuple-element.5.b), custom_call_target="tpu_custom_call" | custom-call | tf_op jit(solution)/shard_map/results/pallas_call | solution.py:586
